TPU v7x, 32 devices: a whole 2x2x4 slice. The times are simulated.
32 devices in a mesh: row: 4 (over x, core), col: 8 (over z, y).
Axes of the slice: x: 2, y: 2, z: 4, core: 2. Of those that a mesh axis runs over, the one named last changes fastest.
Arguments:
- sources: bfloat16 [4096, 768], P(('row', 'col')), may hold values from -2 to 2
- targets: bfloat16 [4096, 768], P(('col', 'row')), may hold values from -2 to 2
- projection: bfloat16 [768, 768], replicated, may hold values from -0.21875 to 0.21875
- language: int32 [4096], replicated, may hold values from 0 to 108
- lang_allow: int32 [109, 109], replicated, may hold values 0 or 1
- tile_allow: int32 [8, 8], replicated, may hold values 0 or 1
Outputs:
- grad_sources: bfloat16 [4096, 768], P(('row', 'col'))
- grad_targets: bfloat16 [4096, 768], P(('col', 'row'))
- grad_proj: float32 [768, 768], replicated
All inputs are finite; a program needn't handle non-finite values.
Results may differ from a plain program's by a relative error of at most 0.0035.
The roundings to bfloat16 on the way count: a program that leaves them out, or rounds other values in their place, can miss the bound.
Values may be sent and summed in bfloat16 or wider, within the bound.
A program may use at most 128 MiB of HBM per device.

v0:
```python
import jax
import jax.numpy as jnp
from jax import lax
from jax.sharding import PartitionSpec as P

TILE = 512


SCALE = 20.0
MARGIN = 0.3


def embedded(inputs, projection):
    raw_proj = jnp.dot(inputs, projection, preferred_element_type=jnp.float32)
    length = jnp.sqrt(jnp.sum(raw_proj * raw_proj, axis=-1, keepdims=True) + 1e-06)
    return (raw_proj, length)


def permitted(row_index, col_index, language, lang_allow, tile_allow):
    tile_cols = jnp.take(tile_allow, col_index // TILE, axis=1)
    tile_ok = jnp.take(tile_cols, row_index // TILE, axis=0)
    row_lang = lax.dynamic_slice_in_dim(language, row_index[0], row_index.shape[0])
    col_lang = lax.dynamic_slice_in_dim(language, col_index[0], col_index.shape[0])
    lang_cols = jnp.take(lang_allow, col_lang, axis=1)
    pair_ok = jnp.take(lang_cols, row_lang, axis=0)
    return (tile_ok * pair_ok == 1) | (row_index[:, None] == col_index[None, :])


def backward_proj(inputs, raw_proj, length, upstream, projection):
    unit_vec = raw_proj / length
    dir_grad = (
        (upstream - unit_vec * jnp.sum(unit_vec * upstream, axis=-1, keepdims=True)) / length
    ).astype(jnp.bfloat16)
    grad_in = jnp.dot(dir_grad, projection.T, preferred_element_type=jnp.float32).astype(
        jnp.bfloat16
    )
    grad_weight = jnp.dot(inputs.T, dir_grad, preferred_element_type=jnp.float32)
    return (grad_in, grad_weight)


def per_device(sources, targets, projection, language, lang_allow, tile_allow):
    src_raw, src_len = embedded(sources, projection)
    tgt_raw, tgt_len = embedded(targets, projection)
    src_unit = (src_raw / src_len).astype(jnp.bfloat16)
    tgt_unit = (tgt_raw / tgt_len).astype(jnp.bfloat16)
    row_emb = lax.all_gather(src_unit, "col", axis=0, tiled=True)
    col_emb = lax.all_gather(tgt_unit, "row", axis=0, tiled=True)
    row_count = row_emb.shape[0]
    col_count = col_emb.shape[0]
    row_begin = lax.axis_index("row") * row_count
    col_begin = lax.axis_index("col") * col_count
    row_index = row_begin + jnp.arange(row_count)
    col_index = col_begin + jnp.arange(col_count)
    allowed = permitted(row_index, col_index, language, lang_allow, tile_allow)
    similar = jnp.dot(row_emb, col_emb.T, preferred_element_type=jnp.float32)
    diagonal = (row_index[:, None] == col_index[None, :]).astype(jnp.float32)
    logits = SCALE * (similar - MARGIN * diagonal)
    weights = jnp.where(allowed, jnp.exp(logits - SCALE), jnp.float32(0.0))
    row_part = jnp.sum(weights, axis=1)
    col_part = jnp.sum(weights, axis=0)
    row_total = lax.psum(row_part, "col")
    col_total = lax.psum(col_part, "row")
    row_lse = jnp.log(row_total) + SCALE
    col_lse = jnp.log(col_total) + SCALE
    soft_rows = jnp.where(allowed, jnp.exp(logits - row_lse[:, None]), jnp.float32(0.0))
    soft_cols = jnp.where(allowed, jnp.exp(logits - col_lse[None, :]), jnp.float32(0.0))
    logit_grad = (SCALE * (0.5 * (soft_rows + soft_cols) - diagonal)).astype(jnp.bfloat16)
    src_terms = jnp.dot(logit_grad, col_emb, preferred_element_type=jnp.float32)
    src_grad = lax.psum_scatter(src_terms, "col", scatter_dimension=0, tiled=True)
    tgt_terms = lax.dot_general(
        logit_grad, row_emb, (((0,), (0,)), ((), ())), preferred_element_type=jnp.float32
    )
    tgt_grad = lax.psum_scatter(tgt_terms, "row", scatter_dimension=0, tiled=True)
    grad_sources, weight_src = backward_proj(sources, src_raw, src_len, src_grad, projection)
    grad_targets, weight_tgt = backward_proj(targets, tgt_raw, tgt_len, tgt_grad, projection)
    grad_proj = lax.psum(weight_src + weight_tgt, ("row", "col"))
    return (grad_sources, grad_targets, grad_proj)


def solution(mesh):
    return jax.shard_map(
        per_device,
        mesh=mesh,
        in_specs=(P(("row", "col"), None), P(("col", "row"), None), P(), P(), P(), P()),
        out_specs=(P(("row", "col"), None), P(("col", "row"), None), P()),
        check_vma=False,
    )
```

profile of v0, /device:TPU:1, one launch (start us, length us, event | category | flops | bytes accessed | tf_op | source)
XLA Modules:
  0.0 346.0 jit_solution(8552331662522744524)
XLA Ops:
  7.2 0.0 copy-start
  7.2 0.0 copy-start.8
  7.2 0.0 copy-start.6
  7.2 0.0 copy-start.7
  7.2 0.0 all-gather.2.cloned.1.call-start
  7.3 1.2 copy-done
  8.4 1.3 multiply_reduce_fusion.3
  9.8 0.8 fusion.14
  10.6 0.0 all-gather.2.cloned.1.call-update
  10.6 0.0 reduce-scatter.5.cloned.1.call-start
  10.7 0.5 slice.7
  12.5 0.5 slice.6
  14.3 0.0 copy-done.8
  14.3 0.1 copy.14
  14.4 0.0 copy-done.6
  14.4 0.1 copy.16
  15.2 0.0 copy-done.7
  15.2 0.1 compare_and_fusion.2
  15.3 1.0 gather_fusion.2
  16.3 0.1 select_bitcast_fusion
  16.5 0.1 copy.17
  16.6 1.0 gather_fusion
  17.7 0.1 select_bitcast_fusion.1
  17.9 0.1 copy.15
  18.6 0.1 fusion.10
  18.7 4.9 %gather_fusion.3 = s32[1024,512]{1,0:T(8,128)} fusion(s32[109,512]{1,0:T(8,128)S(1)} %copy.17, s32[1024]{0:T(1024)S(1)} %fusion.10), kind=kCustom, calls=%fused_computation.3 | custom fusion | bytes 4198400 | tf_op jit(solution)/shard_map/jit(_take)/gather | solution.py:25
  23.6 0.0 copy-start.4
  23.6 4.9 %gather_fusion.1 = s32[1024,512]{1,0:T(8,128)} fusion(s32[8,512]{1,0:T(8,128)S(1)} %copy.15, s32[1024]{0:T(1024)S(1)} %broadcast_clamp_fusion), kind=kCustom, calls=%fused_computation.1 | custom fusion | bytes 4198400 | tf_op jit(solution)/shard_map/jit(_take)/gather | solution.py:21
  28.5 0.1 compare_and_fusion
  28.6 0.0 copy-done.4
  28.6 0.4 multiply_reduce_fusion.2
  29.0 0.1 fusion.15
  29.1 9.9 %all_gather.7 = bf16[512,768]{1,0:T(8,128)(2,1)S(1)} all-gather(bf16[128,768]{1,0:T(8,128)(2,1)S(1)} %fusion.15), channel_id=1, replica_groups=mesh['row'=4,'col'=8] {'row'}, dimensions={0}, use_global_device_ids=true | all-gather | bytes 983040 | tf_op jit(solution)/shard_map/all_gather | solution.py:47
  39.1 0.0 copy-start.1
  39.1 17.3 %all-gather.2.cloned.1.call-done = bf16[1024,768]{1,0:T(8,128)(2,1)} async-done(((bf16[128,768]{1,0:T(8,128)(2,1)}), bf16[1024,768]{1,0:T(8,128)(2,1)}) %all-gather.2.cloned.1.call-update) | async-done | bytes 1572880 | tf_op jit(solution)/shard_map/all_gather | solution.py:46
  56.4 5.2 %fusion.6 = (f32[1024]{0:T(1024)S(1)}, f32[512]{0:T(512)S(1)}, pred[1024,512]{1,0:T(8,128)(4,1)}, f32[1024,512]{1,0:T(8,128)}) fusion(s32[512]{0:T(512)S(1)} %iota_add_fusion.1, s32[1024]{0:T(1024)S(1)} %iota_add_fusion, s32[1024,512]{1,0:T(8,128)} %gather_fusion.3, pred[1024]{0:T(1024)(128)(4,1)S(1)} %get-tuple-element.19, s32[1024,512]{1,0:T(8,128)} %gather_fusion.1, ...), kind=kOutput, calls=%fused_computation.16 | convolution fusion | flops 812120576 | bytes 9189376 | tf_op jit(solution)/shard_map/dot_general | solution.py:55
  61.6 0.0 copy-done.1
  61.6 16.0 %psum.21 = f32[1024]{0:T(1024)S(1)} all-reduce(f32[1024]{0:T(1024)S(1)} %get-tuple-element.9), channel_id=1, replica_groups=mesh['row'=4,'col'=8] {'col'}, use_global_device_ids=true, to_apply=%region_3.4 | all-reduce | flops 1024 | bytes 8192 | tf_op jit(solution)/shard_map/psum | solution.py:61
  77.7 9.5 %psum.22 = f32[512]{0:T(512)S(1)} all-reduce(f32[512]{0:T(512)S(1)} %get-tuple-element.10), channel_id=1, replica_groups=mesh['row'=4,'col'=8] {'row'}, use_global_device_ids=true, to_apply=%region_5.6 | all-reduce | flops 512 | bytes 4096 | tf_op jit(solution)/shard_map/psum | solution.py:62
  87.2 0.0 copy-start.9
  87.2 2.8 fusion.4
  90.0 0.0 copy-done.9
  90.0 2.2 fusion.18
  92.2 0.0 reduce-scatter.5.cloned.1.call-update
  92.2 0.0 reduce-scatter.3.cloned.1.call-start
  92.3 3.8 %fusion.17 = f32[1024,768]{1,0:T(8,128)} fusion(bf16[1024,512]{1,0:T(8,128)(2,1)S(1)} %fusion.4, bf16[512,768]{1,0:T(8,128)(2,1)} %copy-done.1), kind=kOutput, calls=%fused_computation.76 | convolution fusion | flops 805306368 | bytes 4980736 | tf_op jit(solution)/shard_map/dot_general | solution.py:68
  96.0 0.0 copy-start.5
  96.0 0.0 reduce-scatter.3.cloned.1.call-update
  96.1 0.0 all-reduce.2.cloned.1.call-start
  96.1 21.9 %reduce-scatter.5.cloned.1.call-done = f32[128,768]{1,0:T(8,128)} async-done(((f32[512,768]{1,0:T(8,128)}), f32[128,768]{1,0:T(8,128)}) %reduce-scatter.5.cloned.1.call-update) | async-done | bytes 393232 | tf_op jit(solution)/shard_map/reduce_scatter | solution.py:73
  118.0 1.2 multiply_reduce_fusion
  119.2 76.4 %reduce-scatter.3.cloned.1.call-done = f32[128,768]{1,0:T(8,128)} async-done(((f32[1024,768]{1,0:T(8,128)}), f32[128,768]{1,0:T(8,128)}) %reduce-scatter.3.cloned.1.call-update) | async-done | bytes 393232 | tf_op jit(solution)/shard_map/reduce_scatter | solution.py:69
  195.6 1.2 multiply_reduce_fusion.1
  196.8 0.0 copy-done.5
  196.8 1.6 fusion.16
  198.4 0.0 copy-done.2
  198.4 2.0 add_bitcast_fusion
  200.4 0.0 all-reduce.2.cloned.1.call-update
  200.4 0.0 copy-start.3
  200.4 1.2 convolution_convert_fusion
  201.7 0.0 copy-done.3
  201.7 1.2 convolution_convert_fusion.1
  202.9 133.6 %all-reduce.2.cloned.1.call-done = f32[768,768]{0,1:T(8,128)} async-done(((f32[768,768]{0,1:T(8,128)}), f32[768,768]{0,1:T(8,128)}) %all-reduce.2.cloned.1.call-update) | async-done | bytes 2359312 | tf_op jit(solution)/shard_map/psum | solution.py:76
  336.4 3.0 copy.18
  (13 shorter events, 0.1 us)
Async XLA Ops:
  7.2 1.3 copy-start
  7.2 7.1 %copy-start.8 = (s32[8,8]{1,0:T(8,128)S(1)}, s32[8,8]{1,0:T(8,128)}, u32[]{:S(2)}) copy-start(s32[8,8]{1,0:T(8,128)} %param.11) | copy-start | bytes 772
  7.2 7.2 %copy-start.6 = (s32[109,109]{1,0:T(8,128)S(1)}, s32[109,109]{1,0:T(8,128)}, u32[]{:S(2)}) copy-start(s32[109,109]{1,0:T(8,128)} %param.10) | copy-start | bytes 142576
  7.2 8.0 %copy-start.7 = (s32[4096]{0:T(1024)S(1)}, s32[4096]{0:T(1024)}, u32[]{:S(2)}) copy-start(s32[4096]{0:T(1024)} %param.9) | copy-start | bytes 49156
  7.2 49.2 %all-gather.2.cloned.1.call-start = ((), (), s32[]{:S(2)}) async-start(), calls=%async_computation.2 | async-start | bytes 1769472 | tf_op jit(solution)/shard_map/all_gather | solution.py:46
  10.6 107.4 %reduce-scatter.5.cloned.1.call-start = ((), (), s32[]{:S(2)}) async-start(), calls=%async_computation.4 | async-start | bytes 1966080 | tf_op jit(solution)/shard_map/reduce_scatter | solution.py:73
  23.6 5.0 %copy-start.4 = (bf16[128,768]{1,0:T(8,128)(2,1)S(1)}, bf16[128,768]{1,0:T(8,128)(2,1)}, u32[]{:S(2)}) copy-start(bf16[128,768]{1,0:T(8,128)(2,1)} %param.7) | copy-start | bytes 589828
  39.1 22.5 %copy-start.1 = (bf16[512,768]{1,0:T(8,128)(2,1)}, bf16[512,768]{1,0:T(8,128)(2,1)S(1)}, u32[]{:S(2)}) copy-start(bf16[512,768]{1,0:T(8,128)(2,1)S(1)} %all_gather.7) | copy-start | bytes 2359300
  87.2 2.8 copy-start.9
  92.2 103.4 %reduce-scatter.3.cloned.1.call-start = ((), (), s32[]{:S(2)}) async-start(), calls=%async_computation.3 | async-start | bytes 3538944 | tf_op jit(solution)/shard_map/reduce_scatter | solution.py:69
  96.0 100.7 %copy-start.5 = (bf16[128,768]{1,0:T(8,128)(2,1)S(1)}, bf16[128,768]{1,0:T(8,128)(2,1)}, u32[]{:S(2)}) copy-start(bf16[128,768]{1,0:T(8,128)(2,1)} %param.6) | copy-start | bytes 589828
  96.1 240.4 %all-reduce.2.cloned.1.call-start = ((), (), s32[]{:S(2)}) async-start(), calls=%async_computation.5 | async-start | bytes 4718592 | tf_op jit(solution)/shard_map/psum | solution.py:76
  119.2 79.2 %copy-start.2 = (f32[128,768]{1,0:T(8,128)S(1)}, f32[128,768]{1,0:T(8,128)}, u32[]{:S(2)}) copy-start(f32[128,768]{1,0:T(8,128)} %reduce-scatter.5.cloned.1.call-done) | copy-start | bytes 1179652
  200.4 1.2 copy-start.3
Sparse Core Ops, SparseCore 0:
  10.8 45.5 all-gather.1
  92.3 25.6 reduce-scatter.4
  122.0 73.5 reduce-scatter.2
  202.5 133.9 all-reduce.1
where the time goes:
time: 348 us; the launch traced here: 346 us
  waiting for transfers between devices  249 us (72%)
  blocking collectives  35.5 us (10%)
  matrix products  18.9 us (5%)
  between operations  17.9 us (5%)
  local copies, waits for them, and re-layouts  17.5 us (5%)
  other arithmetic  6.71 us (2%)
    psum x1, waiting for transfers between devices, per_device(): grad_proj = lax.psum(weight_src + weight_tgt, ('row', 'col'))  134 us
    reduce_scatter x1, waiting for transfers between devices, per_device(): lax.psum_scatter(src_terms, 'col', scatter_dimension=0, tiled=True)  76.4 us
    reduce_scatter x1, waiting for transfers between devices, per_device(): lax.psum_scatter(tgt_terms, 'row', scatter_dimension=0, tiled=True)  21.9 us
    all_gather x1, waiting for transfers between devices, per_device(): row_emb = lax.all_gather(src_unit, 'col', axis=0, tiled=True)  17.3 us
    psum x1, blocking collectives, per_device(): row_total = lax.psum(row_part, 'col')  16 us
    all_gather x1, blocking collectives, per_device(): col_emb = lax.all_gather(tgt_unit, 'row', axis=0, tiled=True)  9.94 us
    psum x1, blocking collectives, per_device(): col_total = lax.psum(col_part, 'row')  9.5 us
  transfers between devices with their start and end apart: 4, of which 4 were waited for; matrix products, arithmetic and copies ran while one was open for 6% of the time, Pallas kernels for 0%

commit v1 on v0

--- a/solution.py
+++ b/solution.py
@@ -1,13 +1,330 @@
+import functools
+
 import jax
 import jax.numpy as jnp
 from jax import lax
+from jax.experimental import pallas as pl
+from jax.experimental.pallas import tpu as pltpu
 from jax.sharding import PartitionSpec as P
 
 TILE = 512
-
-
+LANES = 128
 SCALE = 20.0
 MARGIN = 0.3
+YN = 2
+BF16 = jnp.bfloat16
+F32 = jnp.float32
+MESH = pl.DeviceIdType.MESH
+
+
+def mm(a, b, ca, cb):
+    return lax.dot_general(a, b, (((ca,), (cb,)), ((), ())), preferred_element_type=F32)
+
+
+def fused(
+    RN, ZN, PR, PC,
+    src_ref, tgt_ref, proj_ref, lang_ref, allow_ref, tile_ref,
+    gsrc_ref, gtgt_ref, gproj_ref,
+    sraw, traw, sun, tun, lang_cols, mask, e_ref, g_ref,
+    rowx, colx, ssend, srecv, tsend, trecv, salong, ralong, talong, qalong,
+    w_ref, wsend, wrecv, zsend, zrecv, zfin, wfin, acc,
+    zs_sem, zr_sem, qs_sem, qr_sem,
+):
+    QN = RN * YN
+    B, D = src_ref.shape
+    cols = QN * B
+    row = lax.axis_index("row")
+    col = lax.axis_index("col")
+    y = lax.rem(col, YN)
+    z = col // YN
+    q = y * RN + row
+    CN = ZN * YN
+
+    def zpeer(d):
+        return lax.rem(z + d, ZN)
+
+    def qpeer(d):
+        return lax.rem(q + d, QN)
+
+    def zdev(t):
+        return (row, t * YN + y)
+
+    def qdev(t):
+        return (lax.rem(t, RN), z * YN + t // RN)
+
+    sends = []
+
+    def zsend_one(k, d, src, dst):
+        t = zpeer(d)
+        c = pltpu.make_async_remote_copy(
+            src, dst, zs_sem.at[k, d], zr_sem.at[k, z], device_id=zdev(t), device_id_type=MESH
+        )
+        c.start()
+        sends.append(c)
+
+    def qsend_one(k, d, src, dst):
+        t = qpeer(d)
+        c = pltpu.make_async_remote_copy(
+            src, dst, qs_sem.at[k, d], qr_sem.at[k, q], device_id=qdev(t), device_id_type=MESH
+        )
+        c.start()
+        sends.append(c)
+
+    def zwait(k, d, buf):
+        t = zpeer(d)
+        pltpu.make_async_remote_copy(
+            buf.at[t], buf.at[t], zs_sem.at[k, d], zr_sem.at[k, t],
+            device_id=zdev(t), device_id_type=MESH,
+        ).wait_recv()
+        return t
+
+    def qwait(k, d, buf):
+        t = qpeer(d)
+        pltpu.make_async_remote_copy(
+            buf.at[t], buf.at[t], qs_sem.at[k, d], qr_sem.at[k, t],
+            device_id=qdev(t), device_id_type=MESH,
+        ).wait_recv()
+        return t
+
+    barrier = pltpu.get_barrier_semaphore()
+    for d in range(1, ZN):
+        pl.semaphore_signal(barrier, inc=1, device_id=zdev(zpeer(d)), device_id_type=MESH)
+    for d in range(1, QN):
+        pl.semaphore_signal(barrier, inc=1, device_id=qdev(qpeer(d)), device_id_type=MESH)
+
+    def embed(inp, raw):
+        r = mm(inp[...], proj_ref[...], 1, 0)
+        raw[...] = r
+        length = jnp.sqrt(jnp.sum(r * r, axis=-1, keepdims=True) + 1e-06)
+        return (r / length).astype(BF16)
+
+    sun[z] = embed(src_ref, sraw)
+    tun[q] = embed(tgt_ref, traw)
+    pl.semaphore_wait(barrier, ZN + QN - 2)
+    for d in range(1, ZN):
+        zsend_one(0, d, sun.at[z], sun.at[z])
+    for d in range(1, QN):
+        qsend_one(0, d, tun.at[q], tun.at[q])
+
+    kind = lax.broadcasted_iota(jnp.int32, (LANES, B), 0)
+
+    def one_hot(block):
+        return jnp.where(kind == lang_ref[pl.ds(block, 1), :], 1.0, 0.0).astype(BF16)
+
+    for t in range(QN):
+        lang_cols[:, t * B : (t + 1) * B] = mm(
+            allow_ref[...], one_hot(z * QN + t), 1, 0
+        ).astype(BF16)
+
+    def diagonal(s):
+        rows = lax.broadcasted_iota(jnp.int32, (B, cols), 0) + (row * CN + s * YN + y) * B
+        colid = lax.broadcasted_iota(jnp.int32, (B, cols), 1) + z * cols
+        return rows == colid
+
+    def mask_step(s, c):
+        sb = row * CN + s * YN + y
+        ok = mm(one_hot(sb), lang_cols[...], 0, 0)
+        for t in range(QN):
+            allow = tile_ref[sb * B // TILE, (z * QN + t) * B // TILE]
+            part = ok[:, t * B : (t + 1) * B]
+            mask[s, :, t * B : (t + 1) * B] = jnp.where(allow == 1, part, 0.0)
+        return c
+
+    lax.fori_loop(0, ZN, mask_step, 0)
+
+    for d in range(1, ZN):
+        zwait(0, d, sun)
+    for d in range(1, QN):
+        qwait(0, d, tun)
+
+    colx[q] = jnp.zeros((1, cols), F32)
+
+    def totals_step(s, c):
+        diag = diagonal(s)
+        sim = mm(sun[s], tun[...].reshape(cols, D), 1, 1)
+        logits = SCALE * (sim - jnp.where(diag, MARGIN, 0.0))
+        e = jnp.where(diag | (mask[s] > 0.5), jnp.exp(logits - SCALE), 0.0)
+        e_ref[s] = e
+        part = e[:, :LANES]
+        for t in range(1, cols // LANES):
+            part += e[:, t * LANES : (t + 1) * LANES]
+        rowx[z, pl.ds(s, 1), :] = jnp.sum(part.T, axis=0, keepdims=True)
+        colx[q] += jnp.sum(e, axis=0, keepdims=True)
+        return c
+
+    lax.fori_loop(0, ZN, totals_step, 0)
+    for d in range(1, ZN):
+        zsend_one(1, d, rowx.at[z], rowx.at[z])
+    for d in range(1, QN):
+        qsend_one(1, d, colx.at[q], colx.at[q])
+    for d in range(1, ZN):
+        zwait(1, d, rowx)
+    for d in range(1, QN):
+        qwait(1, d, colx)
+    row_inv = (0.5 * SCALE) / jnp.sum(rowx[...], axis=0)
+    rowx_inv = acc
+    rowx_inv[0:ZN, 0:B] = row_inv
+    col_inv = (0.5 * SCALE) / jnp.sum(colx[...], axis=0)
+
+    def grad_block(s):
+        inv = rowx_inv[pl.ds(s, 1), 0:B]
+        inv = jnp.broadcast_to(inv, (B, B)).T[:, :1]
+        g = e_ref[s] * (inv + col_inv) - jnp.where(diagonal(s), SCALE, 0.0)
+        g = g.astype(BF16)
+        for t in range(QN):
+            g_ref[t, pl.ds(pl.multiple_of(s * B, B), B), :] = g[:, t * B : (t + 1) * B]
+        return mm(g, tun[...].reshape(cols, D), 1, 0)
+
+    def split(part, unit):
+        u = unit.astype(F32)
+        along = jnp.sum(part * u, axis=-1, keepdims=True)
+        rest = part - along * u
+        return rest.astype(BF16), jnp.broadcast_to(along, (B, B)).T[:1, :]
+
+    for d in range(1, ZN):
+        s = zpeer(d)
+        rest, along = split(grad_block(s), sun[s])
+        ssend[s] = rest
+        salong[s] = along
+        zsend_one(2, d, ssend.at[s], srecv.at[z])
+        zsend_one(5, d, salong.at[s], ralong.at[z])
+    src_grad = grad_block(z)
+    for d in range(1, QN):
+        t = qpeer(d)
+        rest, along = split(mm(g_ref[t], sun[...].reshape(ZN * B, D), 0, 0), tun[t])
+        tsend[t] = rest
+        talong[t] = along
+        qsend_one(2, d, tsend.at[t], trecv.at[q])
+        qsend_one(5, d, talong.at[t], qalong.at[q])
+    tgt_grad = mm(g_ref[q], sun[...].reshape(ZN * B, D), 0, 0)
+
+    def direction(raw, grad):
+        r = raw[...]
+        length = jnp.sqrt(jnp.sum(r * r, axis=-1, keepdims=True) + 1e-06)
+        unit = r / length
+        return (
+            (grad - unit * jnp.sum(unit * grad, axis=-1, keepdims=True)) / length
+        ).astype(BF16)
+
+    def along_unit(along, unit):
+        return jnp.broadcast_to(along, (B, B)).T[:, :1] * unit.astype(F32)
+
+    along = jnp.zeros((1, B), F32)
+    for d in range(1, QN):
+        t = qwait(2, d, trecv)
+        qwait(5, d, qalong)
+        tgt_grad += trecv[t].astype(F32)
+        along += qalong[t]
+    tgt_grad += along_unit(along, tun[q])
+    tgt_dir = direction(traw, tgt_grad)
+    along = jnp.zeros((1, B), F32)
+    for d in range(1, ZN):
+        s = zwait(2, d, srecv)
+        zwait(5, d, ralong)
+        src_grad += srecv[s].astype(F32)
+        along += ralong[s]
+    src_grad += along_unit(along, sun[z])
+    src_dir = direction(sraw, src_grad)
+
+    w_ref[...] = mm(
+        jnp.concatenate([src_ref[...], tgt_ref[...]], axis=0),
+        jnp.concatenate([src_dir, tgt_dir], axis=0),
+        0, 0,
+    )
+    W = D // QN
+    for d in range(1, QN):
+        t = qpeer(d)
+        wsend[t] = w_ref[pl.ds(pl.multiple_of(t * W, 16), W), :].astype(BF16)
+        qsend_one(3, d, wsend.at[t], wrecv.at[q])
+    gsrc_ref[...] = mm(src_dir, proj_ref[...], 1, 1).astype(BF16)
+    gtgt_ref[...] = mm(tgt_dir, proj_ref[...], 1, 1).astype(BF16)
+    total = w_ref[pl.ds(pl.multiple_of(q * W, 16), W), :]
+    for d in range(1, QN):
+        t = qwait(3, d, wrecv)
+        total += wrecv[t].astype(F32)
+    HR, HC = W // PR, D // PC
+    for p in range(ZN):
+        a, b = p // PC, p % PC
+        zsend[p] = total[a * HR : (a + 1) * HR, b * HC : (b + 1) * HC]
+    for d in range(1, ZN):
+        s = zpeer(d)
+        zsend_one(3, d, zsend.at[s], zrecv.at[z])
+    piece = zsend[z]
+    for d in range(1, ZN):
+        s = zwait(3, d, zrecv)
+        piece += zrecv[s]
+    zfin[z] = piece.astype(BF16)
+    for d in range(1, ZN):
+        zsend_one(4, d, zfin.at[z], zfin.at[z])
+    for d in range(1, ZN):
+        zwait(4, d, zfin)
+    for p in range(ZN):
+        a, b = p // PC, p % PC
+        wfin[q, a * HR : (a + 1) * HR, b * HC : (b + 1) * HC] = zfin[p]
+    for d in range(1, QN):
+        qsend_one(4, d, wfin.at[q], wfin.at[q])
+    gproj_ref[pl.ds(pl.multiple_of(q * W, 16), W), :] = wfin[q].astype(F32)
+    for d in range(1, QN):
+        t = qwait(4, d, wfin)
+        gproj_ref[pl.ds(pl.multiple_of(t * W, 16), W), :] = wfin[t].astype(F32)
+    for c in sends:
+        c.wait_send()
+
+
+def fused_device(RN, CN, PR, PC, sources, targets, projection, language, lang_allow, tile_allow):
+    ZN, QN = CN // YN, RN * YN
+    B, D = sources.shape
+    W = D // QN
+    pad = LANES - lang_allow.shape[0]
+    allow = jnp.pad(lang_allow.astype(BF16), ((0, pad), (0, pad)))
+    vmem = pl.BlockSpec(memory_space=pltpu.VMEM)
+    smem = pl.BlockSpec(memory_space=pltpu.SMEM)
+    V = pltpu.VMEM
+    return pl.pallas_call(
+        functools.partial(fused, RN, ZN, PR, PC),
+        out_shape=(
+            jax.ShapeDtypeStruct((B, D), BF16),
+            jax.ShapeDtypeStruct((B, D), BF16),
+            jax.ShapeDtypeStruct((D, D), F32),
+        ),
+        in_specs=[vmem] * 5 + [smem],
+        out_specs=(vmem,) * 3,
+        scratch_shapes=[
+            V((B, D), F32),
+            V((B, D), F32),
+            V((ZN, B, D), BF16),
+            V((QN, B, D), BF16),
+            V((LANES, QN * B), BF16),
+            V((ZN, B, QN * B), F32),
+            V((ZN, B, QN * B), F32),
+            V((QN, ZN * B, B), BF16),
+            V((ZN, ZN, B), F32),
+            V((QN, 1, QN * B), F32),
+            V((ZN, B, D), BF16),
+            V((ZN, B, D), BF16),
+            V((QN, B, D), BF16),
+            V((QN, B, D), BF16),
+            V((ZN, 1, B), F32),
+            V((ZN, 1, B), F32),
+            V((QN, 1, B), F32),
+            V((QN, 1, B), F32),
+            V((D, D), F32),
+            V((QN, W, D), BF16),
+            V((QN, W, D), BF16),
+            V((ZN, W // PR, D // PC), F32),
+            V((ZN, W // PR, D // PC), F32),
+            V((ZN, W // PR, D // PC), BF16),
+            V((QN, W, D), BF16),
+            V((8, B), F32),
+            pltpu.SemaphoreType.DMA((6, ZN)),
+            pltpu.SemaphoreType.DMA((6, ZN)),
+            pltpu.SemaphoreType.DMA((6, QN)),
+            pltpu.SemaphoreType.DMA((6, QN)),
+        ],
+        compiler_params=pltpu.CompilerParams(
+            collective_id=0, has_side_effects=True, vmem_limit_bytes=48 * 2**20
+        ),
+    )(sources, targets, projection, language.reshape(-1, B), allow, tile_allow)
 
 
 def embedded(inputs, projection):
@@ -77,9 +394,28 @@
     return (grad_sources, grad_targets, grad_proj)
 
 
+def pieces(ZN, W, D):
+    for PR in (1, 2, 4):
+        if ZN % PR == 0 and W % (16 * PR) == 0 and D % (LANES * (ZN // PR)) == 0:
+            return PR, ZN // PR
+    return None
+
+
 def solution(mesh):
+    RN, CN = mesh.shape["row"], mesh.shape["col"]
+
+    def device(sources, targets, projection, language, lang_allow, tile_allow):
+        B, D = sources.shape
+        split = None
+        if CN % YN == 0 and D % (16 * RN * YN) == 0 and B == LANES and RN * CN <= 64:
+            split = pieces(CN // YN, D // (RN * YN), D)
+        args = (sources, targets, projection, language, lang_allow, tile_allow)
+        if split is None or lang_allow.shape[0] > LANES:
+            return per_device(*args)
+        return fused_device(RN, CN, *split, *args)
+
     return jax.shard_map(
-        per_device,
+        device,
         mesh=mesh,
         in_specs=(P(("row", "col"), None), P(("col", "row"), None), P(), P(), P(), P()),
         out_specs=(P(("row", "col"), None), P(("col", "row"), None), P()),

time: 348 us -> 103 us (0.30)
  waiting for transfers between devices: 249 us -> 0 us
  Pallas kernels: 0 us -> 94 us
  blocking collectives: 35.5 us -> 0 us
  matrix products: 18.9 us -> 0 us
  between operations: 17.9 us -> 0.65 us
  local copies, waits for them, and re-layouts: 17.5 us -> 7.3 us
  other arithmetic: 6.71 us -> 0.83 us
    psum x1 -> x0, waiting for transfers between devices: 134 us -> none  [per_device(): grad_proj = lax.psum(weight_src + weight_tgt, ('row', 'col'))]
    reduce_scatter x2 -> x0, waiting for transfers between devices: 98.3 us -> none  [the longest x1 76.4 us: per_device(): lax.psum_scatter(src_terms, 'col', scatter_dimension=0, tiled=True)]
    pallas_call x0 -> x1, Pallas kernels: none -> 94 us  [fused_device(): pl.pallas_call(functools.partial(fused, RN, ZN, PR, PC), out_shape=(jax.S...]
    psum x2 -> x0, blocking collectives: 25.5 us -> none  [the longest x1 16 us: per_device(): row_total = lax.psum(row_part, 'col')]
    dot_general x9 -> x0, matrix products: 18.9 us -> none  [the longest x1 5.2 us: per_device(): similar = jnp.dot(row_emb, col_emb.T, preferred_element_type=jnp.float32)]
    all_gather x1 -> x0, waiting for transfers between devices: 17.3 us -> none  [per_device(): row_emb = lax.all_gather(src_unit, 'col', axis=0, tiled=True)]
    gather x4 -> x0, local copies, waits for them, and re-layouts: 11.8 us -> none  [the longest x1 4.89 us: permitted(): tile_ok = jnp.take(tile_cols, row_index // TILE, axis=0)]
    all_gather x1 -> x0, blocking collectives: 9.94 us -> none  [per_device(): col_emb = lax.all_gather(tgt_unit, 'row', axis=0, tiled=True)]
  transfers between devices with their start and end apart: 4 -> 0, of which waited for: 4 -> 0; matrix products, arithmetic and copies ran while one was open for 6% -> 0% of each run, Pallas kernels for 0% -> 0%
where the time goes in v1:
time: 103 us
  Pallas kernels  94 us (91%)
  local copies, waits for them, and re-layouts  7.3 us (7%)
    pallas_call x1, Pallas kernels, fused_device(): pl.pallas_call(functools.partial(fused, RN, ZN, PR, PC), out_shape=(jax.S...  94 us
    unnamed x13, local copies, waits for them, and re-layouts  7.28 us

profile of v1, /device:TPU:1, one launch (start us, length us, event | category | flops | bytes accessed | tf_op | source)
XLA Modules:
  0.0 102.8 jit_solution(10067478306729437923)
XLA Ops:
  0.6 0.8 convert_element_type.5
  1.5 0.0 copy-start
  1.5 1.3 %copy-done = bf16[768,768]{1,0:T(8,128)(2,1)S(1)} copy-done((bf16[768,768]{1,0:T(8,128)(2,1)S(1)}, bf16[768,768]{1,0:T(8,128)(2,1)}, u32[]{:S(2)}) %copy-start) | copy-done | bytes 1179672
  2.7 0.0 copy-start.1
  2.7 0.9 copy-done.1
  3.7 0.0 copy-start.2
  3.7 0.9 copy-done.2
  4.6 0.0 copy-start.3
  4.6 0.7 copy-done.3
  5.3 0.0 copy-start.4
  5.3 0.7 copy-done.4
  6.0 94.0 %shard_map.85 = (bf16[128,768]{1,0:T(8,128)(2,1)S(1)}, bf16[128,768]{1,0:T(8,128)(2,1)S(1)}, f32[768,768]{1,0:T(8,128)S(1)}) custom-call(bf16[128,768]{1,0:T(8,128)(2,1)S(1)} %copy-done.1, bf16[128,768]{1,0:T(8,128)(2,1)S(1)} %copy-done.2, bf16[768,768]{1,0:T(8,128)(2,1)S(1)} %copy-done, s32[32,128]{1,0:T(8,128)S(1)} %bitcast.1, ...), custom_call_target="tpu_custom_call" | custom-call | tf_op jit(solution)/shard_map/pallas_call | solution.py:283
  100.0 0.7 copy.12
  100.7 0.7 copy.13
  101.4 1.4 %copy.14 = f32[768,768]{1,0:T(8,128)} copy(f32[768,768]{1,0:T(8,128)S(1)} %get-tuple-element.8) | data formatting | bytes 4718592
  (1 shorter events, 0.0 us)
Async XLA Ops:
  1.5 1.3 %copy-start = (bf16[768,768]{1,0:T(8,128)(2,1)S(1)}, bf16[768,768]{1,0:T(8,128)(2,1)}, u32[]{:S(2)}) copy-start(bf16[768,768]{1,0:T(8,128)(2,1)} %proj_ref.1) | copy-start | bytes 3538948
  2.7 0.9 copy-start.1
  3.7 0.9 copy-start.2
  4.6 0.7 copy-start.3
  5.3 0.7 copy-start.4

commit v2 on v1

v2 whole, which is shorter than its diff:
```python
import functools

import jax
import jax.numpy as jnp
from jax import lax
from jax.experimental import pallas as pl
from jax.experimental.pallas import tpu as pltpu
from jax.sharding import PartitionSpec as P

TILE = 512
LANES = 128
SCALE = 20.0
MARGIN = 0.3
YN = 2
CORES = 2
BF16 = jnp.bfloat16
F32 = jnp.float32
MESH = pl.DeviceIdType.MESH


def mm(a, b, ca, cb):
    return lax.dot_general(a, b, (((ca,), (cb,)), ((), ())), preferred_element_type=F32)


def fused(
    RN, ZN, PR, PC,
    src_hbm, tgt_hbm, proj_hbm, lang_hbm, allow_hbm, tile_ref,
    gsrc_hbm, gtgt_hbm, gproj_hbm,
    src_ref, tgt_ref, proj_ref, lang_ref, allow_ref, gsrc_ref, gtgt_ref,
    sraw, traw, sun, tun, lang_cols, mask, e_ref, g_ref,
    rowx, row_inv, colx, ssend, srecv, tcs, tcr, tsend, trecv, salong, ralong, talong, qalong,
    w_ref, wcr, wsend, wrecv, zpart, zsend, zrecv, wfin,
    loc_sem, zs_sem, zr_sem, qs_sem, qr_sem, js_sem, jr_sem, cs_sem, cr_sem,
    fs_sem, fr_sem, hs_sem, hr_sem, out_sem,
):
    QN = RN * YN
    XN = RN // CORES
    JN = XN * YN
    CN = ZN * YN
    B, D = src_ref.shape
    cols = QN * B
    W = D // QN
    HR, HC = W // PR, D // PC
    row = lax.axis_index("row")
    col = lax.axis_index("col")
    y = lax.rem(col, YN)
    z = col // YN
    q = y * RN + row
    core = lax.rem(row, CORES)
    other = 1 - core
    jme = y * XN + row // CORES

    def zpeer(d):
        return lax.rem(z + d, ZN)

    def qpeer(d):
        return lax.rem(q + d, QN)

    def jpeer(d):
        return lax.rem(jme + d, JN)

    def slot(j, c):
        return (j // XN) * RN + lax.rem(j, XN) * CORES + c

    def zdev(t):
        return (row, t * YN + y)

    def qdev(t):
        return (lax.rem(t, RN), z * YN + t // RN)

    def jdev(j):
        return (lax.rem(j, XN) * CORES + core, z * YN + j // XN)

    sibling = (row + 1 - 2 * core, col)

    sends = []

    def push(src, dst, s_sem, r_sem, dev):
        c = pltpu.make_async_remote_copy(src, dst, s_sem, r_sem, device_id=dev, device_id_type=MESH)
        c.start()
        sends.append(c)

    def arrive(buf, s_sem, r_sem, dev):
        pltpu.make_async_remote_copy(
            buf, buf, s_sem, r_sem, device_id=dev, device_id_type=MESH
        ).wait_recv()

    def zpush(k, d, src, dst):
        push(src, dst, zs_sem.at[k, d], zr_sem.at[k, z], zdev(zpeer(d)))

    def zwait(k, d, buf):
        t = zpeer(d)
        arrive(buf, zs_sem.at[k, d], zr_sem.at[k, t], zdev(t))

    def jpush(k, d, src, dst):
        push(src, dst, js_sem.at[k, d], jr_sem.at[k, jme], jdev(jpeer(d)))

    def jwait(k, d, buf):
        j = jpeer(d)
        arrive(buf, js_sem.at[k, d], jr_sem.at[k, j], jdev(j))

    def cpush(k, j, src, dst):
        push(src, dst, cs_sem.at[k, j], cr_sem.at[k, j], sibling)

    def cwait(k, j, buf):
        arrive(buf, cs_sem.at[k, j], cr_sem.at[k, j], sibling)

    barrier = pltpu.get_barrier_semaphore()
    for d in range(1, ZN):
        pl.semaphore_signal(barrier, inc=1, device_id=zdev(zpeer(d)), device_id_type=MESH)
    for d in range(1, QN):
        pl.semaphore_signal(barrier, inc=1, device_id=qdev(qpeer(d)), device_id_type=MESH)
    loads = [
        pltpu.make_async_copy(a, b, loc_sem.at[k])
        for k, (a, b) in enumerate(
            [
                (src_hbm, src_ref), (proj_hbm, proj_ref), (tgt_hbm, tgt_ref),
                (lang_hbm, lang_ref), (allow_hbm, allow_ref),
            ]
        )
    ]
    for c in loads:
        c.start()

    stores = []

    def store(src, dst, sem):
        c = pltpu.make_async_copy(src, dst, sem)
        c.start()
        stores.append(c)

    def embed(inp, raw):
        r = mm(inp[...], proj_ref[...], 1, 0)
        raw[...] = r
        length = jnp.sqrt(jnp.sum(r * r, axis=-1, keepdims=True) + 1e-06)
        return (r / length).astype(BF16)

    loads[0].wait()
    loads[1].wait()
    sun[z] = embed(src_ref, sraw)
    pl.semaphore_wait(barrier, ZN + QN - 2)
    for d in range(1, ZN):
        zpush(0, d, sun.at[z], sun.at[z])
    loads[2].wait()
    tun[q] = embed(tgt_ref, traw)
    for d in range(1, JN):
        jpush(0, d, tun.at[q], tun.at[q])
    cpush(0, jme, tun.at[q], tun.at[q])

    loads[3].wait()
    loads[4].wait()
    NL = allow_ref.shape[0]
    kind = lax.broadcasted_iota(jnp.int32, (NL, B), 0)
    allow = allow_ref[...].astype(F32).astype(BF16)

    def one_hot(block):
        return jnp.where(kind == lang_ref[pl.ds(block, 1), :], 1.0, 0.0).astype(BF16)

    for t in range(QN):
        lang_cols[:, t * B : (t + 1) * B] = mm(allow, one_hot(z * QN + t), 1, 0).astype(BF16)

    def diagonal(s):
        rows = lax.broadcasted_iota(jnp.int32, (B, cols), 0) + (row * CN + s * YN + y) * B
        colid = lax.broadcasted_iota(jnp.int32, (B, cols), 1) + z * cols
        return rows == colid

    def mask_step(s, c):
        sb = row * CN + s * YN + y
        ok = mm(one_hot(sb), lang_cols[...], 0, 0)
        for t in range(QN):
            tile_ok = tile_ref[sb * B // TILE, (z * QN + t) * B // TILE]
            part = ok[:, t * B : (t + 1) * B]
            mask[s, :, t * B : (t + 1) * B] = jnp.where(tile_ok == 1, part, 0.0)
        return c

    lax.fori_loop(0, ZN, mask_step, 0)

    for d in range(1, JN):
        j = jpeer(d)
        t = slot(j, core)
        jwait(0, d, tun.at[t])
        cpush(0, j, tun.at[t], tun.at[t])
    for d in range(JN):
        j = jpeer(d)
        cwait(0, j, tun.at[slot(j, other)])

    colx[q] = jnp.zeros((1, cols), F32)

    def totals(s):
        diag = diagonal(s)
        sim = mm(sun[s], tun[...].reshape(cols, D), 1, 1)
        logits = SCALE * (sim - jnp.where(diag, MARGIN, 0.0))
        e = jnp.where(diag | (mask[s] > 0.5), jnp.exp(logits - SCALE), 0.0)
        e_ref[s] = e
        part = e[:, :LANES]
        for t in range(1, cols // LANES):
            part += e[:, t * LANES : (t + 1) * LANES]
        rowx[z, pl.ds(s, 1), :] = jnp.sum(part.T, axis=0, keepdims=True)
        colx[q] += jnp.sum(e, axis=0, keepdims=True)

    for d in range(ZN):
        s = zpeer(d)
        if d:
            zwait(0, d, sun.at[s])
        totals(s)
    for d in range(1, ZN):
        zpush(1, d, rowx.at[z], rowx.at[z])
    for d in range(1, QN):
        push(colx.at[q], colx.at[q], qs_sem.at[d], qr_sem.at[q], qdev(qpeer(d)))
    for d in range(1, ZN):
        zwait(1, d, rowx.at[zpeer(d)])
    for d in range(1, QN):
        t = qpeer(d)
        arrive(colx.at[t], qs_sem.at[d], qr_sem.at[t], qdev(t))
    row_inv[...] = (0.5 * SCALE) / jnp.sum(rowx[...], axis=0)
    col_inv = (0.5 * SCALE) / jnp.sum(colx[...], axis=0)

    def grad_block(s):
        inv = jnp.broadcast_to(row_inv[pl.ds(s, 1), :], (B, B)).T[:, :1]
        g = e_ref[s] * (inv + col_inv) - jnp.where(diagonal(s), SCALE, 0.0)
        g = g.astype(BF16)
        for t in range(QN):
            g_ref[t, pl.ds(pl.multiple_of(s * B, B), B), :] = g[:, t * B : (t + 1) * B]
        return mm(g, tun[...].reshape(cols, D), 1, 0)

    def split(part, unit):
        u = unit.astype(F32)
        along = jnp.sum(part * u, axis=-1, keepdims=True)
        rest = part - along * u
        return rest.astype(BF16), jnp.broadcast_to(along, (B, B)).T[:1, :]

    def along_unit(along, unit):
        return jnp.broadcast_to(along, (B, B)).T[:, :1] * unit.astype(F32)

    for d in range(1, ZN):
        s = zpeer(d)
        rest, along = split(grad_block(s), sun[s])
        ssend[s] = rest
        salong[s] = along
        zpush(2, d, ssend.at[s], srecv.at[z])
        zpush(5, d, salong.at[s], ralong.at[z])
    src_grad = grad_block(z)

    def tgt_part(t):
        return mm(g_ref[t], sun[...].reshape(ZN * B, D), 0, 0)

    for d in range(1, JN + 1):
        j = jpeer(d)
        tcs[j] = tgt_part(slot(j, other))
        cpush(1, j, tcs.at[j], tcr.at[j])
    for d in range(1, JN):
        j = jpeer(d)
        t = slot(j, core)
        part = tgt_part(t)
        cwait(1, j, tcr.at[j])
        rest, along = split(part + tcr[j], tun[t])
        tsend[j] = rest
        talong[j] = along
        jpush(1, d, tsend.at[j], trecv.at[jme])
        jpush(2, d, talong.at[j], qalong.at[jme])
    tgt_grad = tgt_part(q)
    cwait(1, jme, tcr.at[jme])
    tgt_grad += tcr[jme]

    def direction(raw, grad):
        r = raw[...]
        length = jnp.sqrt(jnp.sum(r * r, axis=-1, keepdims=True) + 1e-06)
        unit = r / length
        return (
            (grad - unit * jnp.sum(unit * grad, axis=-1, keepdims=True)) / length
        ).astype(BF16)

    along = jnp.zeros((1, B), F32)
    for d in range(1, JN):
        j = jpeer(d)
        jwait(1, d, trecv.at[j])
        jwait(2, d, qalong.at[j])
        tgt_grad += trecv[j].astype(F32)
        along += qalong[j]
    tgt_grad += along_unit(along, tun[q])
    tgt_dir = direction(traw, tgt_grad)
    w_ref[...] = mm(tgt_ref[...], tgt_dir, 0, 0)
    gtgt_ref[...] = mm(tgt_dir, proj_ref[...], 1, 1).astype(BF16)
    store(gtgt_ref, gtgt_hbm, loc_sem.at[5])

    along = jnp.zeros((1, B), F32)
    for d in range(1, ZN):
        s = zpeer(d)
        zwait(2, d, srecv.at[s])
        zwait(5, d, ralong.at[s])
        src_grad += srecv[s].astype(F32)
        along += ralong[s]
    src_grad += along_unit(along, sun[z])
    src_dir = direction(sraw, src_grad)

    w_ref[...] += mm(src_ref[...], src_dir, 0, 0)

    def rows_of(t):
        return pl.ds(pl.multiple_of(t * W, 16), W)

    for d in range(1, JN + 1):
        j = jpeer(d)
        cpush(2, j, w_ref.at[rows_of(slot(j, other))], wcr.at[j])
    gsrc_ref[...] = mm(src_dir, proj_ref[...], 1, 1).astype(BF16)
    store(gsrc_ref, gsrc_hbm, loc_sem.at[6])
    for d in range(1, JN):
        j = jpeer(d)
        cwait(2, j, wcr.at[j])
        wsend[j] = (w_ref[rows_of(slot(j, core)), :] + wcr[j]).astype(BF16)
        jpush(3, d, wsend.at[j], wrecv.at[jme])
    cwait(2, jme, wcr.at[jme])
    total = w_ref[rows_of(q), :] + wcr[jme]
    for d in range(1, JN):
        j = jpeer(d)
        jwait(3, d, wrecv.at[j])
        total += wrecv[j].astype(F32)
    for p in range(ZN):
        a, b = p // PC, p % PC
        zpart[p] = total[a * HR : (a + 1) * HR, b * HC : (b + 1) * HC]
    for d in range(1, ZN):
        s = zpeer(d)
        zsend[s] = zpart[s].astype(BF16)
        zpush(3, d, zsend.at[s], zrecv.at[z])
    piece = zpart[z]
    for d in range(1, ZN):
        s = zpeer(d)
        zwait(3, d, zrecv.at[s])
        piece += zrecv[s].astype(F32)
    wfin[q, z] = piece.astype(BF16)
    for d in range(1, ZN):
        zpush(4, d, wfin.at[q, z], wfin.at[q, z])

    def put(t, p):
        r = pl.ds(pl.multiple_of(t * W + (p // PC) * HR, 16), HR)
        c = pl.ds(pl.multiple_of(lax.rem(p, PC) * HC, LANES), HC)
        store(wfin.at[t, p], gproj_hbm.at[r, c], out_sem.at[t, p])

    for k in range(ZN):
        p = zpeer(k)
        if k:
            zwait(4, k, wfin.at[q, p])
        here = wfin.at[q, p]
        for d in range(1, JN):
            push(here, here, fs_sem.at[d, p], fr_sem.at[jme, p], jdev(jpeer(d)))
        push(here, here, hs_sem.at[jme, p], hr_sem.at[jme, p], sibling)
        put(q, p)
    for k in range(ZN):
        p = zpeer(k)
        for d in range(1, JN):
            j = jpeer(d)
            t = slot(j, core)
            here = wfin.at[t, p]
            arrive(here, fs_sem.at[d, p], fr_sem.at[j, p], jdev(j))
            push(here, here, hs_sem.at[j, p], hr_sem.at[j, p], sibling)
            put(t, p)
    for k in range(ZN):
        p = zpeer(k)
        for d in range(JN):
            j = jpeer(d)
            t = slot(j, other)
            arrive(wfin.at[t, p], hs_sem.at[j, p], hr_sem.at[j, p], sibling)
            put(t, p)
    for c in sends:
        c.wait_send()
    for c in stores:
        c.wait()


def fused_device(RN, CN, PR, PC, sources, targets, projection, language, lang_allow, tile_allow):
    ZN, QN, JN = CN // YN, RN * YN, RN * YN // CORES
    B, D = sources.shape
    NL = lang_allow.shape[0]
    W = D // QN
    langs = language.reshape(-1, B)
    smem = pl.BlockSpec(memory_space=pltpu.SMEM)
    hbm = pl.BlockSpec(memory_space=pltpu.HBM)
    V = pltpu.VMEM
    S = pltpu.SemaphoreType.DMA
    piece = (ZN, W // PR, D // PC)
    grad_sources, grad_targets, grad_proj = pl.pallas_call(
        functools.partial(fused, RN, ZN, PR, PC),
        out_shape=(
            jax.ShapeDtypeStruct((B, D), BF16),
            jax.ShapeDtypeStruct((B, D), BF16),
            jax.ShapeDtypeStruct((D, D), BF16),
        ),
        in_specs=[hbm] * 5 + [smem],
        out_specs=(hbm,) * 3,
        scratch_shapes=[
            V((B, D), BF16),
            V((B, D), BF16),
            V((D, D), BF16),
            V(langs.shape, jnp.int32),
            V((NL, NL), jnp.int32),
            V((B, D), BF16),
            V((B, D), BF16),
            V((B, D), F32),
            V((B, D), F32),
            V((ZN, B, D), BF16),
            V((QN, B, D), BF16),
            V((NL, QN * B), BF16),
            V((ZN, B, QN * B), F32),
            V((ZN, B, QN * B), F32),
            V((QN, ZN * B, B), BF16),
            V((ZN, ZN, B), F32),
            V((ZN, B), F32),
            V((QN, 1, QN * B), F32),
            V((ZN, B, D), BF16),
            V((ZN, B, D), BF16),
            V((JN, B, D), F32),
            V((JN, B, D), F32),
            V((JN, B, D), BF16),
            V((JN, B, D), BF16),
            V((ZN, 1, B), F32),
            V((ZN, 1, B), F32),
            V((JN, 1, B), F32),
            V((JN, 1, B), F32),
            V((D, D), F32),
            V((JN, W, D), F32),
            V((JN, W, D), BF16),
            V((JN, W, D), BF16),
            V(piece, F32),
            V(piece, BF16),
            V(piece, BF16),
            V((QN, *piece), BF16),
            S((7,)),
            S((6, ZN)),
            S((6, ZN)),
            S((QN,)),
            S((QN,)),
            S((4, JN)),
            S((4, JN)),
            S((3, JN)),
            S((3, JN)),
            S((JN, ZN)),
            S((JN, ZN)),
            S((JN, ZN)),
            S((JN, ZN)),
            S((QN, ZN)),
        ],
        compiler_params=pltpu.CompilerParams(
            collective_id=0, has_side_effects=True, vmem_limit_bytes=60 * 2**20
        ),
    )(sources, targets, projection, langs, lang_allow, tile_allow)
    return grad_sources, grad_targets, grad_proj.astype(F32)


def embedded(inputs, projection):
    raw_proj = jnp.dot(inputs, projection, preferred_element_type=jnp.float32)
    length = jnp.sqrt(jnp.sum(raw_proj * raw_proj, axis=-1, keepdims=True) + 1e-06)
    return (raw_proj, length)


def permitted(row_index, col_index, language, lang_allow, tile_allow):
    tile_cols = jnp.take(tile_allow, col_index // TILE, axis=1)
    tile_ok = jnp.take(tile_cols, row_index // TILE, axis=0)
    row_lang = lax.dynamic_slice_in_dim(language, row_index[0], row_index.shape[0])
    col_lang = lax.dynamic_slice_in_dim(language, col_index[0], col_index.shape[0])
    lang_cols = jnp.take(lang_allow, col_lang, axis=1)
    pair_ok = jnp.take(lang_cols, row_lang, axis=0)
    return (tile_ok * pair_ok == 1) | (row_index[:, None] == col_index[None, :])


def backward_proj(inputs, raw_proj, length, upstream, projection):
    unit_vec = raw_proj / length
    dir_grad = (
        (upstream - unit_vec * jnp.sum(unit_vec * upstream, axis=-1, keepdims=True)) / length
    ).astype(jnp.bfloat16)
    grad_in = jnp.dot(dir_grad, projection.T, preferred_element_type=jnp.float32).astype(
        jnp.bfloat16
    )
    grad_weight = jnp.dot(inputs.T, dir_grad, preferred_element_type=jnp.float32)
    return (grad_in, grad_weight)


def per_device(sources, targets, projection, language, lang_allow, tile_allow):
    src_raw, src_len = embedded(sources, projection)
    tgt_raw, tgt_len = embedded(targets, projection)
    src_unit = (src_raw / src_len).astype(jnp.bfloat16)
    tgt_unit = (tgt_raw / tgt_len).astype(jnp.bfloat16)
    row_emb = lax.all_gather(src_unit, "col", axis=0, tiled=True)
    col_emb = lax.all_gather(tgt_unit, "row", axis=0, tiled=True)
    row_count = row_emb.shape[0]
    col_count = col_emb.shape[0]
    row_begin = lax.axis_index("row") * row_count
    col_begin = lax.axis_index("col") * col_count
    row_index = row_begin + jnp.arange(row_count)
    col_index = col_begin + jnp.arange(col_count)
    allowed = permitted(row_index, col_index, language, lang_allow, tile_allow)
    similar = jnp.dot(row_emb, col_emb.T, preferred_element_type=jnp.float32)
    diagonal = (row_index[:, None] == col_index[None, :]).astype(jnp.float32)
    logits = SCALE * (similar - MARGIN * diagonal)
    weights = jnp.where(allowed, jnp.exp(logits - SCALE), jnp.float32(0.0))
    row_part = jnp.sum(weights, axis=1)
    col_part = jnp.sum(weights, axis=0)
    row_total = lax.psum(row_part, "col")
    col_total = lax.psum(col_part, "row")
    row_lse = jnp.log(row_total) + SCALE
    col_lse = jnp.log(col_total) + SCALE
    soft_rows = jnp.where(allowed, jnp.exp(logits - row_lse[:, None]), jnp.float32(0.0))
    soft_cols = jnp.where(allowed, jnp.exp(logits - col_lse[None, :]), jnp.float32(0.0))
    logit_grad = (SCALE * (0.5 * (soft_rows + soft_cols) - diagonal)).astype(jnp.bfloat16)
    src_terms = jnp.dot(logit_grad, col_emb, preferred_element_type=jnp.float32)
    src_grad = lax.psum_scatter(src_terms, "col", scatter_dimension=0, tiled=True)
    tgt_terms = lax.dot_general(
        logit_grad, row_emb, (((0,), (0,)), ((), ())), preferred_element_type=jnp.float32
    )
    tgt_grad = lax.psum_scatter(tgt_terms, "row", scatter_dimension=0, tiled=True)
    grad_sources, weight_src = backward_proj(sources, src_raw, src_len, src_grad, projection)
    grad_targets, weight_tgt = backward_proj(targets, tgt_raw, tgt_len, tgt_grad, projection)
    grad_proj = lax.psum(weight_src + weight_tgt, ("row", "col"))
    return (grad_sources, grad_targets, grad_proj)


def pieces(ZN, W, D):
    for PR in (1, 2, 4):
        if ZN % PR == 0 and W % (16 * PR) == 0 and D % (LANES * (ZN // PR)) == 0:
            return PR, ZN // PR
    return None


def solution(mesh):
    RN, CN = mesh.shape["row"], mesh.shape["col"]

    def device(sources, targets, projection, language, lang_allow, tile_allow):
        B, D = sources.shape
        split = None
        if CN % YN == 0 and RN % CORES == 0 and D % (16 * RN * YN) == 0 and B == LANES and RN * CN <= 64:
            split = pieces(CN // YN, D // (RN * YN), D)
        args = (sources, targets, projection, language, lang_allow, tile_allow)
        if split is None:
            return per_device(*args)
        return fused_device(RN, CN, *split, *args)

    return jax.shard_map(
        device,
        mesh=mesh,
        in_specs=(P(("row", "col"), None), P(("col", "row"), None), P(), P(), P(), P()),
        out_specs=(P(("row", "col"), None), P(("col", "row"), None), P()),
        check_vma=False,
    )
```

time: 103 us -> 83.4 us (0.81)
  Pallas kernels: 94 us -> 78.1 us
  local copies, waits for them, and re-layouts: 7.3 us -> 1.36 us
  other arithmetic: 0.83 us -> 2.9 us
    pallas_call x1, Pallas kernels: 94 us -> 78.1 us  [fused_device(): pl.pallas_call(functools.partial(fused, RN, ZN, PR, PC), out_shape=(jax.S...]
    unnamed x13 -> x6, local copies, waits for them, and re-layouts: 7.28 us -> 1.36 us
    convert_element_type x1, other arithmetic: 0.83 us -> 2.9 us  [fused_device(): return (grad_sources, grad_targets, grad_proj.astype(F32))]
where the time goes in v2:
time: 83.4 us; the launch traced here: 83 us
  Pallas kernels  78.1 us (94%)
  other arithmetic  2.9 us (3%)
  local copies, waits for them, and re-layouts  1.36 us (2%)
    pallas_call x1, Pallas kernels, fused_device(): pl.pallas_call(functools.partial(fused, RN, ZN, PR, PC), out_shape=(jax.S...  78.1 us
    convert_element_type x1, other arithmetic, fused_device(): return (grad_sources, grad_targets, grad_proj.astype(F32))  2.9 us

profile of v2, /device:TPU:1, one launch (start us, length us, event | category | flops | bytes accessed | tf_op | source)
XLA Modules:
  0.0 83.0 jit_solution(10957244888858261755)
XLA Ops:
  0.6 78.1 %shard_map.85 = (bf16[128,768]{1,0:T(8,128)(2,1)}, bf16[128,768]{1,0:T(8,128)(2,1)}, bf16[768,768]{1,0:T(8,128)(2,1)}) custom-call(bf16[128,768]{1,0:T(8,128)(2,1)} %src_hbm.1, bf16[128,768]{1,0:T(8,128)(2,1)} %tgt_hbm.1, bf16[768,768]{1,0:T(8,128)(2,1)} %proj_hbm.1, s32[32,128]{1,0:T(8,128)} %bitcast.1, s32[109,109]{1,0:T(8,128)} %allow_hbm.1, s32[8,8]{1,0:T(8,128)} %tile_ref.1), custom_call_target="tpu_custom_call" | custom-call | tf_op jit(solution)/shard_map/pallas_call | solution.py:380
  78.8 0.0 copy-start.1
  78.8 0.0 copy-start
  78.8 2.9 %convert_element_type.3 = f32[768,768]{1,0:T(8,128)} convert(bf16[768,768]{1,0:T(8,128)(2,1)} %get-tuple-element.8) | non-fusion elementwise | flops 589824 | bytes 3538944 | tf_op jit(solution)/shard_map/convert_element_type | solution.py:445
  81.7 0.0 copy-done.1
  81.7 0.7 copy.11
  82.4 0.0 copy-done
  82.4 0.7 copy.12
Async XLA Ops:
  78.8 2.9 %copy-start.1 = (bf16[128,768]{1,0:T(8,128)(2,1)S(1)}, bf16[128,768]{1,0:T(8,128)(2,1)}, u32[]{:S(2)}) copy-start(bf16[128,768]{1,0:T(8,128)(2,1)} %get-tuple-element.12) | copy-start | bytes 589828
  78.8 3.6 %copy-start = (bf16[128,768]{1,0:T(8,128)(2,1)S(1)}, bf16[128,768]{1,0:T(8,128)(2,1)}, u32[]{:S(2)}) copy-start(bf16[128,768]{1,0:T(8,128)(2,1)} %get-tuple-element.13) | copy-start | bytes 589828

commit v3 on v2

--- a/solution.py
+++ b/solution.py
@@ -13,6 +13,7 @@
 MARGIN = 0.3
 YN = 2
 CORES = 2
+PARTS = 4
 BF16 = jnp.bfloat16
 F32 = jnp.float32
 MESH = pl.DeviceIdType.MESH
@@ -32,6 +33,7 @@
     w_ref, wcr, wsend, wrecv, zpart, zsend, zrecv, wfin,
     loc_sem, zs_sem, zr_sem, qs_sem, qr_sem, js_sem, jr_sem, cs_sem, cr_sem,
     fs_sem, fr_sem, hs_sem, hr_sem, out_sem,
+    hold, hold_along, passed, passed_along, src_acc, along_acc, rs_sem, rr_sem,
 ):
     QN = RN * YN
     XN = RN // CORES
@@ -75,18 +77,36 @@
 
     sends = []
 
-    def push(src, dst, s_sem, r_sem, dev):
+    def push(src, dst, s_sem, r_sem, dev, cond=None):
         c = pltpu.make_async_remote_copy(src, dst, s_sem, r_sem, device_id=dev, device_id_type=MESH)
-        c.start()
-        sends.append(c)
+        if cond is None:
+            c.start()
+        else:
+            pl.when(cond)(c.start)
+        sends.append((c, cond))
 
     def arrive(buf, s_sem, r_sem, dev):
         pltpu.make_async_remote_copy(
             buf, buf, s_sem, r_sem, device_id=dev, device_id_type=MESH
         ).wait_recv()
 
-    def zpush(k, d, src, dst):
-        push(src, dst, zs_sem.at[k, d], zr_sem.at[k, z], zdev(zpeer(d)))
+    last = ZN - 1
+    relays = ZN == 4
+
+    def far(t):
+        return ((z == 0) & (t == last)) | ((z == last) & (t == 0))
+
+    def middle(t):
+        return ((z == last - 1) & (t == 0)) | ((z == 1) & (t == last))
+
+    def no(c):
+        return jnp.logical_not(c)
+
+    near_first = sorted(range(1, ZN), key=lambda d: abs(2 * d - ZN))
+    far_first = near_first[::-1]
+
+    def zpush(k, d, src, dst, cond=None):
+        push(src, dst, zs_sem.at[k, d], zr_sem.at[k, z], zdev(zpeer(d)), cond)
 
     def zwait(k, d, buf):
         t = zpeer(d)
@@ -139,8 +159,8 @@
     loads[1].wait()
     sun[z] = embed(src_ref, sraw)
     pl.semaphore_wait(barrier, ZN + QN - 2)
-    for d in range(1, ZN):
-        zpush(0, d, sun.at[z], sun.at[z])
+    for d in near_first:
+        zpush(0, d, sun.at[z], sun.at[z], no(far(zpeer(d))) if relays else None)
     loads[2].wait()
     tun[q] = embed(tgt_ref, traw)
     for d in range(1, JN):
@@ -198,10 +218,26 @@
         rowx[z, pl.ds(s, 1), :] = jnp.sum(part.T, axis=0, keepdims=True)
         colx[q] += jnp.sum(e, axis=0, keepdims=True)
 
-    for d in range(ZN):
+    totals(z)
+    if relays:
+        d = near_first[0]
         s = zpeer(d)
-        if d:
-            zwait(0, d, sun.at[s])
+        pl.when(middle(s))(functools.partial(zwait, 0, d, sun.at[s]))
+        push(sun.at[s], sun.at[s], rs_sem.at[2], zr_sem.at[0, s], zdev(last - s), middle(s))
+        first = 1 + lax.rem(z, 2)
+        final = last * (1 - z // 2)
+        order = [first, last * 2 - z - first - final, final]
+    else:
+        order = [zpeer(d) for d in range(1, ZN)]
+
+    def take(s):
+        arrive(sun.at[s], zs_sem.at[0, 1], zr_sem.at[0, s], zdev(s))
+
+    for k, s in enumerate(order):
+        if relays and k == len(order) - 1:
+            pl.when(no(middle(s)))(functools.partial(take, s))
+        else:
+            take(s)
         totals(s)
     for d in range(1, ZN):
         zpush(1, d, rowx.at[z], rowx.at[z])
@@ -232,13 +268,33 @@
     def along_unit(along, unit):
         return jnp.broadcast_to(along, (B, B)).T[:, :1] * unit.astype(F32)
 
-    for d in range(1, ZN):
+    def send_sources(d, cond=None):
         s = zpeer(d)
-        rest, along = split(grad_block(s), sun[s])
-        ssend[s] = rest
+        zpush(2, d, ssend.at[s], srecv.at[z], cond)
+        zpush(5, d, salong.at[s], ralong.at[z], cond)
+
+    for d in far_first:
+        s = zpeer(d)
+        part = grad_block(s)
+        u = sun[s].astype(F32)
+        along = jnp.sum(part * u, axis=-1, keepdims=True)
+        rest = part - along * u
+        along = jnp.broadcast_to(along, (B, B)).T[:1, :]
+        ssend[s] = rest.astype(BF16)
         salong[s] = along
-        zpush(2, d, ssend.at[s], srecv.at[z])
-        zpush(5, d, salong.at[s], ralong.at[z])
+        if not relays:
+            send_sources(d)
+        elif d == near_first[0]:
+            hold[...] = rest
+            hold_along[...] = along
+            send_sources(d, no(middle(s)))
+        else:
+            send_sources(d, no(far(s)))
+            by = z + 1 - 2 * lax.rem(z, 2)
+            if d in (1, last):
+                k = 0 if d == 1 else 3
+                push(ssend.at[s], passed, rs_sem.at[k], rr_sem.at[0], zdev(by), far(s))
+                push(salong.at[s], passed_along, rs_sem.at[k + 1], rr_sem.at[1], zdev(by), far(s))
     src_grad = grad_block(z)
 
     def tgt_part(t):
@@ -248,6 +304,19 @@
         j = jpeer(d)
         tcs[j] = tgt_part(slot(j, other))
         cpush(1, j, tcs.at[j], tcr.at[j])
+    if relays:
+        d = near_first[0]
+        s = zpeer(d)
+
+        @pl.when(middle(s))
+        def _():
+            end = zdev(last - s)
+            arrive(passed, rs_sem.at[0], rr_sem.at[0], end)
+            arrive(passed_along, rs_sem.at[1], rr_sem.at[1], end)
+            ssend[s] = (hold[...] + passed[...].astype(F32)).astype(BF16)
+            salong[s] = hold_along[...] + passed_along[...]
+
+        send_sources(d, middle(s))
     for d in range(1, JN):
         j = jpeer(d)
         t = slot(j, core)
@@ -283,14 +352,22 @@
     gtgt_ref[...] = mm(tgt_dir, proj_ref[...], 1, 1).astype(BF16)
     store(gtgt_ref, gtgt_hbm, loc_sem.at[5])
 
-    along = jnp.zeros((1, B), F32)
+    src_acc[...] = src_grad
+    along_acc[...] = jnp.zeros((1, B), F32)
     for d in range(1, ZN):
         s = zpeer(d)
-        zwait(2, d, srecv.at[s])
-        zwait(5, d, ralong.at[s])
-        src_grad += srecv[s].astype(F32)
-        along += ralong[s]
-    src_grad += along_unit(along, sun[z])
+
+        def add(d=d, s=s):
+            zwait(2, d, srecv.at[s])
+            zwait(5, d, ralong.at[s])
+            src_acc[...] += srecv[s].astype(F32)
+            along_acc[...] += ralong[s]
+
+        if relays:
+            pl.when(no(far(s)))(add)
+        else:
+            add()
+    src_grad = src_acc[...] + along_unit(along_acc[...], sun[z])
     src_dir = direction(sraw, src_grad)
 
     w_ref[...] += mm(src_ref[...], src_dir, 0, 0)
@@ -360,9 +437,36 @@
             t = slot(j, other)
             arrive(wfin.at[t, p], hs_sem.at[j, p], hr_sem.at[j, p], sibling)
             put(t, p)
-    for c in sends:
-        c.wait_send()
+    for c, cond in sends:
+        if cond is None:
+            c.wait_send()
+        else:
+            pl.when(cond)(c.wait_send)
     for c in stores:
+        c.wait()
+
+
+def finish(gs_in, gt_in, gp_in, gs_out, gt_out, gp_out, low, wide, whole_sem, in_sem, out_sem):
+    rows = low.shape[1]
+    whole = [
+        pltpu.make_async_copy(a, b, whole_sem.at[k])
+        for k, (a, b) in enumerate([(gs_in, gs_out), (gt_in, gt_out)])
+    ]
+    loads = [
+        pltpu.make_async_copy(gp_in.at[pl.ds(k * rows, rows), :], low.at[k], in_sem.at[k])
+        for k in range(PARTS)
+    ]
+    stores = [
+        pltpu.make_async_copy(wide.at[k], gp_out.at[pl.ds(k * rows, rows), :], out_sem.at[k])
+        for k in range(PARTS)
+    ]
+    for c in loads + whole:
+        c.start()
+    for k in range(PARTS):
+        loads[k].wait()
+        wide[k] = low[k].astype(F32)
+        stores[k].start()
+    for c in whole + stores:
         c.wait()
 
 
@@ -437,12 +541,38 @@
             S((JN, ZN)),
             S((JN, ZN)),
             S((QN, ZN)),
+            V((B, D), F32),
+            V((1, B), F32),
+            V((B, D), BF16),
+            V((1, B), F32),
+            V((B, D), F32),
+            V((1, B), F32),
+            S((5,)),
+            S((2,)),
         ],
         compiler_params=pltpu.CompilerParams(
             collective_id=0, has_side_effects=True, vmem_limit_bytes=60 * 2**20
         ),
     )(sources, targets, projection, langs, lang_allow, tile_allow)
-    return grad_sources, grad_targets, grad_proj.astype(F32)
+    rows = D // PARTS
+    return pl.pallas_call(
+        finish,
+        out_shape=(
+            jax.ShapeDtypeStruct((B, D), BF16),
+            jax.ShapeDtypeStruct((B, D), BF16),
+            jax.ShapeDtypeStruct((D, D), F32),
+        ),
+        in_specs=[hbm] * 3,
+        out_specs=(hbm,) * 3,
+        scratch_shapes=[
+            V((PARTS, rows, D), BF16),
+            V((PARTS, rows, D), F32),
+            S((2,)),
+            S((PARTS,)),
+            S((PARTS,)),
+        ],
+        compiler_params=pltpu.CompilerParams(vmem_limit_bytes=60 * 2**20),
+    )(grad_sources, grad_targets, grad_proj)
 
 
 def embedded(inputs, projection):

time: 83.4 us -> 93.6 us (1.12)
  Pallas kernels: 78.1 us -> 92.8 us
  other arithmetic: 2.9 us -> 0 us
  local copies, waits for them, and re-layouts: 1.36 us -> 0 us
    pallas_call x0 -> x1, Pallas kernels: none -> 13.1 us  [fused_device(): pl.pallas_call(finish, out_shape=(jax.ShapeDtypeStruct((B, D), BF16), jax...]
    convert_element_type x1 -> x0, other arithmetic: 2.9 us -> none  [fused_device(): return (grad_sources, grad_targets, grad_proj.astype(F32))]
    pallas_call x1, Pallas kernels: 78.1 us -> 79.7 us  [fused_device(): pl.pallas_call(functools.partial(fused, RN, ZN, PR, PC), out_shape=(jax.S...]
    unnamed x6 -> x0, local copies, waits for them, and re-layouts: 1.36 us -> none
where the time goes in v3:
time: 93.6 us; the launch traced here: 93.4 us
  Pallas kernels  92.8 us (99%)
    pallas_call x1, Pallas kernels, fused_device(): pl.pallas_call(functools.partial(fused, RN, ZN, PR, PC), out_shape=(jax.S...  79.7 us
    pallas_call x1, Pallas kernels, fused_device(): pl.pallas_call(finish, out_shape=(jax.ShapeDtypeStruct((B, D), BF16), jax...  13.1 us

profile of v3, /device:TPU:1, one launch (start us, length us, event | category | flops | bytes accessed | tf_op | source)
XLA Modules:
  0.0 93.4 jit_solution(912276868774675113)
XLA Ops:
  0.6 79.7 %shard_map.85 = (bf16[128,768]{1,0:T(8,128)(2,1)}, bf16[128,768]{1,0:T(8,128)(2,1)}, bf16[768,768]{1,0:T(8,128)(2,1)}) custom-call(bf16[128,768]{1,0:T(8,128)(2,1)} %src_hbm.1, bf16[128,768]{1,0:T(8,128)(2,1)} %tgt_hbm.1, bf16[768,768]{1,0:T(8,128)(2,1)} %proj_hbm.1, s32[32,128]{1,0:T(8,128)} %bitcast.1, s32[109,109]{1,0:T(8,128)} %allow_hbm.1, s32[8,8]{1,0:T(8,128)} %tile_ref.1), custom_call_target="tpu_custom_call" | custom-call | tf_op jit(solution)/shard_map/pallas_call | solution.py:484
  80.3 13.1 %shard_map.86 = (bf16[128,768]{1,0:T(8,128)(2,1)}, bf16[128,768]{1,0:T(8,128)(2,1)}, f32[768,768]{1,0:T(8,128)}) custom-call(bf16[128,768]{1,0:T(8,128)(2,1)} %get-tuple-element.6.gs_in, bf16[128,768]{1,0:T(8,128)(2,1)} %get-tuple-element.7.gt_in, bf16[768,768]{1,0:T(8,128)(2,1)} %get-tuple-element.8.gp_in), custom_call_target="tpu_custom_call" | custom-call | tf_op jit(solution)/shard_map/pallas_call | solution.py:558

commit v4 on v3

--- a/solution.py
+++ b/solution.py
@@ -102,8 +102,12 @@
     def no(c):
         return jnp.logical_not(c)
 
-    near_first = sorted(range(1, ZN), key=lambda d: abs(2 * d - ZN))
-    far_first = near_first[::-1]
+    opposite = last - z
+    scatter_c = 2 * z + 1 - 5 * (z // 2)
+    scatter_b = last - scatter_c
+
+    def zpush_to(k, s, src, dst, cond=None):
+        push(src, dst, zs_sem.at[k, s], zr_sem.at[k, z], zdev(s), cond)
 
     def zpush(k, d, src, dst, cond=None):
         push(src, dst, zs_sem.at[k, d], zr_sem.at[k, z], zdev(zpeer(d)), cond)
@@ -159,8 +163,14 @@
     loads[1].wait()
     sun[z] = embed(src_ref, sraw)
     pl.semaphore_wait(barrier, ZN + QN - 2)
-    for d in near_first:
-        zpush(0, d, sun.at[z], sun.at[z], no(far(zpeer(d))) if relays else None)
+    at_end = (z == 0) | (z == last)
+    if relays:
+        for s in (scatter_b, scatter_c):
+            zpush_to(0, s, sun.at[z], sun.at[z])
+        across, _ = sends.pop()
+    else:
+        for d in range(1, ZN):
+            zpush(0, d, sun.at[z], sun.at[z])
     loads[2].wait()
     tun[q] = embed(tgt_ref, traw)
     for d in range(1, JN):
@@ -200,6 +210,9 @@
         t = slot(j, core)
         jwait(0, d, tun.at[t])
         cpush(0, j, tun.at[t], tun.at[t])
+    if relays:
+        across.wait_send()
+        zpush_to(0, opposite, sun.at[z], sun.at[z], no(at_end))
     for d in range(JN):
         j = jpeer(d)
         cwait(0, j, tun.at[slot(j, other)])
@@ -220,10 +233,11 @@
 
     totals(z)
     if relays:
-        d = near_first[0]
-        s = zpeer(d)
-        pl.when(middle(s))(functools.partial(zwait, 0, d, sun.at[s]))
-        push(sun.at[s], sun.at[s], rs_sem.at[2], zr_sem.at[0, s], zdev(last - s), middle(s))
+        s = scatter_c
+        pl.when(no(at_end))(
+            lambda: arrive(sun.at[s], zs_sem.at[0, s], zr_sem.at[0, s], zdev(s))
+        )
+        push(sun.at[s], sun.at[s], rs_sem.at[2], zr_sem.at[0, s], zdev(last - s), no(at_end))
         first = 1 + lax.rem(z, 2)
         final = last * (1 - z // 2)
         order = [first, last * 2 - z - first - final, final]
@@ -268,33 +282,33 @@
     def along_unit(along, unit):
         return jnp.broadcast_to(along, (B, B)).T[:, :1] * unit.astype(F32)
 
-    def send_sources(d, cond=None):
-        s = zpeer(d)
-        zpush(2, d, ssend.at[s], srecv.at[z], cond)
-        zpush(5, d, salong.at[s], ralong.at[z], cond)
-
-    for d in far_first:
-        s = zpeer(d)
+    def source_part(s):
         part = grad_block(s)
         u = sun[s].astype(F32)
         along = jnp.sum(part * u, axis=-1, keepdims=True)
-        rest = part - along * u
-        along = jnp.broadcast_to(along, (B, B)).T[:1, :]
+        return part - along * u, jnp.broadcast_to(along, (B, B)).T[:1, :]
+
+    def send_sources(s, cond=None):
+        zpush_to(2, s, ssend.at[s], srecv.at[z], cond)
+        zpush_to(5, s, salong.at[s], ralong.at[z], cond)
+
+    for s in (opposite, scatter_b, scatter_c) if relays else [zpeer(d) for d in range(1, ZN)]:
+        rest, along = source_part(s)
         ssend[s] = rest.astype(BF16)
         salong[s] = along
         if not relays:
-            send_sources(d)
-        elif d == near_first[0]:
+            send_sources(s)
+        elif s is opposite:
+            send_sources(s, no(at_end))
+            by = zdev(z + 1 - 2 * lax.rem(z, 2))
+            push(salong.at[s], passed_along, rs_sem.at[1], rr_sem.at[1], by, at_end)
+            push(ssend.at[s], passed, rs_sem.at[0], rr_sem.at[0], by, at_end)
+            to_pass, _ = sends.pop()
+        elif s is scatter_b:
+            send_sources(s, no(at_end))
+        else:
             hold[...] = rest
             hold_along[...] = along
-            send_sources(d, no(middle(s)))
-        else:
-            send_sources(d, no(far(s)))
-            by = z + 1 - 2 * lax.rem(z, 2)
-            if d in (1, last):
-                k = 0 if d == 1 else 3
-                push(ssend.at[s], passed, rs_sem.at[k], rr_sem.at[0], zdev(by), far(s))
-                push(salong.at[s], passed_along, rs_sem.at[k + 1], rr_sem.at[1], zdev(by), far(s))
     src_grad = grad_block(z)
 
     def tgt_part(t):
@@ -305,18 +319,19 @@
         tcs[j] = tgt_part(slot(j, other))
         cpush(1, j, tcs.at[j], tcr.at[j])
     if relays:
-        d = near_first[0]
-        s = zpeer(d)
-
-        @pl.when(middle(s))
+        s = scatter_c
+
+        @pl.when(no(at_end))
         def _():
-            end = zdev(last - s)
-            arrive(passed, rs_sem.at[0], rr_sem.at[0], end)
-            arrive(passed_along, rs_sem.at[1], rr_sem.at[1], end)
+            dev = zdev(opposite)
+            arrive(passed, rs_sem.at[0], rr_sem.at[0], dev)
+            arrive(passed_along, rs_sem.at[1], rr_sem.at[1], dev)
             ssend[s] = (hold[...] + passed[...].astype(F32)).astype(BF16)
             salong[s] = hold_along[...] + passed_along[...]
 
-        send_sources(d, middle(s))
+        pl.when(at_end)(to_pass.wait_send)
+        send_sources(scatter_b, at_end)
+        send_sources(s)
     for d in range(1, JN):
         j = jpeer(d)
         t = slot(j, core)
@@ -446,11 +461,14 @@
         c.wait()
 
 
-def finish(gs_in, gt_in, gp_in, gs_out, gt_out, gp_out, low, wide, whole_sem, in_sem, out_sem):
+def finish(gs_in, gt_in, gp_in, gs_out, gt_out, gp_out, low, wide, held, whole_sem, in_sem, out_sem):
     rows = low.shape[1]
-    whole = [
-        pltpu.make_async_copy(a, b, whole_sem.at[k])
-        for k, (a, b) in enumerate([(gs_in, gs_out), (gt_in, gt_out)])
+    whole_in = [
+        pltpu.make_async_copy(a, held.at[k], whole_sem.at[k]) for k, a in enumerate([gs_in, gt_in])
+    ]
+    whole_out = [
+        pltpu.make_async_copy(held.at[k], b, whole_sem.at[2 + k])
+        for k, b in enumerate([gs_out, gt_out])
     ]
     loads = [
         pltpu.make_async_copy(gp_in.at[pl.ds(k * rows, rows), :], low.at[k], in_sem.at[k])
@@ -460,13 +478,16 @@
         pltpu.make_async_copy(wide.at[k], gp_out.at[pl.ds(k * rows, rows), :], out_sem.at[k])
         for k in range(PARTS)
     ]
-    for c in loads + whole:
+    for c in loads + whole_in:
         c.start()
     for k in range(PARTS):
         loads[k].wait()
         wide[k] = low[k].astype(F32)
         stores[k].start()
-    for c in whole + stores:
+    for k in range(2):
+        whole_in[k].wait()
+        whole_out[k].start()
+    for c in whole_out + stores:
         c.wait()
 
 
@@ -567,7 +588,8 @@
         scratch_shapes=[
             V((PARTS, rows, D), BF16),
             V((PARTS, rows, D), F32),
-            S((2,)),
+            V((2, B, D), BF16),
+            S((4,)),
             S((PARTS,)),
             S((PARTS,)),
         ],

time: 93.6 us -> 79.3 us (0.85)
  Pallas kernels: 92.8 us -> 78.5 us
    pallas_call x1, Pallas kernels: 13.1 us -> 2.63 us  [fused_device(): pl.pallas_call(finish, out_shape=(jax.ShapeDtypeStruct((B, D), BF16), jax...]
    pallas_call x1, Pallas kernels: 79.7 us -> 75.8 us  [fused_device(): pl.pallas_call(functools.partial(fused, RN, ZN, PR, PC), out_shape=(jax.S...]
where the time goes in v4:
time: 79.3 us; the launch traced here: 79.1 us
  Pallas kernels  78.5 us (99%)
    pallas_call x1, Pallas kernels, fused_device(): pl.pallas_call(functools.partial(fused, RN, ZN, PR, PC), out_shape=(jax.S...  75.8 us
    pallas_call x1, Pallas kernels, fused_device(): pl.pallas_call(finish, out_shape=(jax.ShapeDtypeStruct((B, D), BF16), jax...  2.63 us

profile of v4, /device:TPU:1, one launch (start us, length us, event | category | flops | bytes accessed | tf_op | source)
XLA Modules:
  0.0 79.1 jit_solution(5317031455953000347)
XLA Ops:
  0.6 75.8 %shard_map.85 = (bf16[128,768]{1,0:T(8,128)(2,1)}, bf16[128,768]{1,0:T(8,128)(2,1)}, bf16[768,768]{1,0:T(8,128)(2,1)}) custom-call(bf16[128,768]{1,0:T(8,128)(2,1)} %src_hbm.1, bf16[128,768]{1,0:T(8,128)(2,1)} %tgt_hbm.1, bf16[768,768]{1,0:T(8,128)(2,1)} %proj_hbm.1, s32[32,128]{1,0:T(8,128)} %bitcast.1, s32[109,109]{1,0:T(8,128)} %allow_hbm.1, s32[8,8]{1,0:T(8,128)} %tile_ref.1), custom_call_target="tpu_custom_call" | custom-call | tf_op jit(solution)/shard_map/pallas_call | solution.py:505
  76.5 2.6 %shard_map.86 = (bf16[128,768]{1,0:T(8,128)(2,1)}, bf16[128,768]{1,0:T(8,128)(2,1)}, f32[768,768]{1,0:T(8,128)}) custom-call(bf16[128,768]{1,0:T(8,128)(2,1)} %get-tuple-element.6.gs_in, bf16[128,768]{1,0:T(8,128)(2,1)} %get-tuple-element.7.gt_in, bf16[768,768]{1,0:T(8,128)(2,1)} %get-tuple-element.8.gp_in), custom_call_target="tpu_custom_call" | custom-call | tf_op jit(solution)/shard_map/pallas_call | solution.py:579

commit v5 on v4

--- a/solution.py
+++ b/solution.py
@@ -30,7 +30,7 @@
     src_ref, tgt_ref, proj_ref, lang_ref, allow_ref, gsrc_ref, gtgt_ref,
     sraw, traw, sun, tun, lang_cols, mask, e_ref, g_ref,
     rowx, row_inv, colx, ssend, srecv, tcs, tcr, tsend, trecv, salong, ralong, talong, qalong,
-    w_ref, wcr, wsend, wrecv, zpart, zsend, zrecv, wfin,
+    w_ref, wcs, wcr, wsend, wrecv, zpart, zsend, zrecv, wfin,
     loc_sem, zs_sem, zr_sem, qs_sem, qr_sem, js_sem, jr_sem, cs_sem, cr_sem,
     fs_sem, fr_sem, hs_sem, hr_sem, out_sem,
     hold, hold_along, passed, passed_along, src_acc, along_acc, rs_sem, rr_sem,
@@ -211,7 +211,8 @@
         jwait(0, d, tun.at[t])
         cpush(0, j, tun.at[t], tun.at[t])
     if relays:
-        across.wait_send()
+        pl.when(no(at_end))(across.wait_send)
+        sends.append((across, at_end))
         zpush_to(0, opposite, sun.at[z], sun.at[z], no(at_end))
     for d in range(JN):
         j = jpeer(d)
@@ -392,16 +393,17 @@
 
     for d in range(1, JN + 1):
         j = jpeer(d)
-        cpush(2, j, w_ref.at[rows_of(slot(j, other))], wcr.at[j])
+        wcs[j] = w_ref[rows_of(slot(j, other)), :].astype(BF16)
+        cpush(2, j, wcs.at[j], wcr.at[j])
     gsrc_ref[...] = mm(src_dir, proj_ref[...], 1, 1).astype(BF16)
     store(gsrc_ref, gsrc_hbm, loc_sem.at[6])
     for d in range(1, JN):
         j = jpeer(d)
         cwait(2, j, wcr.at[j])
-        wsend[j] = (w_ref[rows_of(slot(j, core)), :] + wcr[j]).astype(BF16)
+        wsend[j] = (w_ref[rows_of(slot(j, core)), :] + wcr[j].astype(F32)).astype(BF16)
         jpush(3, d, wsend.at[j], wrecv.at[jme])
     cwait(2, jme, wcr.at[jme])
-    total = w_ref[rows_of(q), :] + wcr[jme]
+    total = w_ref[rows_of(q), :] + wcr[jme].astype(F32)
     for d in range(1, JN):
         j = jpeer(d)
         jwait(3, d, wrecv.at[j])
@@ -541,7 +543,8 @@
             V((JN, 1, B), F32),
             V((JN, 1, B), F32),
             V((D, D), F32),
-            V((JN, W, D), F32),
+            V((JN, W, D), BF16),
+            V((JN, W, D), BF16),
             V((JN, W, D), BF16),
             V((JN, W, D), BF16),
             V(piece, F32),

time: 79.3 us -> 78.9 us (level)
  no operation moved by 1% of the time
where the time goes in v5:
time: 78.9 us; the launch traced here: 78.7 us
  Pallas kernels  78.1 us (99%)
    pallas_call x1, Pallas kernels, fused_device(): pl.pallas_call(functools.partial(fused, RN, ZN, PR, PC), out_shape=(jax.S...  75.4 us
    pallas_call x1, Pallas kernels, fused_device(): pl.pallas_call(finish, out_shape=(jax.ShapeDtypeStruct((B, D), BF16), jax...  2.63 us

profile of v5, /device:TPU:1, one launch (start us, length us, event | category | flops | bytes accessed | tf_op | source)
XLA Modules:
  0.0 78.7 jit_solution(13356795205819222274)
XLA Ops:
  0.6 75.4 %shard_map.85 = (bf16[128,768]{1,0:T(8,128)(2,1)}, bf16[128,768]{1,0:T(8,128)(2,1)}, bf16[768,768]{1,0:T(8,128)(2,1)}) custom-call(bf16[128,768]{1,0:T(8,128)(2,1)} %src_hbm.1, bf16[128,768]{1,0:T(8,128)(2,1)} %tgt_hbm.1, bf16[768,768]{1,0:T(8,128)(2,1)} %proj_hbm.1, s32[32,128]{1,0:T(8,128)} %bitcast.1, s32[109,109]{1,0:T(8,128)} %allow_hbm.1, s32[8,8]{1,0:T(8,128)} %tile_ref.1), custom_call_target="tpu_custom_call" | custom-call | tf_op jit(solution)/shard_map/pallas_call | solution.py:507
  76.1 2.6 %shard_map.86 = (bf16[128,768]{1,0:T(8,128)(2,1)}, bf16[128,768]{1,0:T(8,128)(2,1)}, f32[768,768]{1,0:T(8,128)}) custom-call(bf16[128,768]{1,0:T(8,128)(2,1)} %get-tuple-element.6.gs_in, bf16[128,768]{1,0:T(8,128)(2,1)} %get-tuple-element.7.gt_in, bf16[768,768]{1,0:T(8,128)(2,1)} %get-tuple-element.8.gp_in), custom_call_target="tpu_custom_call" | custom-call | tf_op jit(solution)/shard_map/pallas_call | solution.py:582
